TPU v7x, 512 devices: a whole 4x4x16 slice. The times are simulated.
512 devices in a mesh: ctx: 128 (over x, z, core), head: 4 (over y).
Axes of the slice: x: 4, y: 4, z: 16, core: 2. Of those that a mesh axis runs over, the one named last changes fastest.
Arguments:
- queries: bfloat16 [16, 32768, 128], P('head', 'ctx'), may hold values from -6 to 6
- key_vectors: bfloat16 [16, 32768, 128], P('head', 'ctx'), may hold values from -6 to 6
- value_vectors: bfloat16 [16, 32768, 128], P('head', 'ctx'), may hold values from -12 to 12
- norm_gain: float32 [16, 128], P('head'), may hold values from 0.5 to 1.5
- upstream: bfloat16 [16, 32768, 128], P('head', 'ctx'), may hold values from -6 to 6
- cluster_ids: int32 [16, 32768, 1], P('head', 'ctx'), may hold values from 0 to 255; in each aligned block of 256 rows (0 to 255, 256 to 511, ..., all dimensions but the last counted through in order) at most 2 rows name the same one
- positions: int32 [32768], P('ctx'), may hold values from 0 to 32767, each once
Outputs:
- normed_out: bfloat16 [16, 32768, 128], P('head', 'ctx')
- grad_queries: bfloat16 [16, 32768, 128], P('head', 'ctx')
- grad_keys: bfloat16 [16, 32768, 128], P('head', 'ctx')
- grad_values: bfloat16 [16, 32768, 128], P('head', 'ctx')
- centroids: float32 [256, 16, 128], P('ctx', 'head')
Inputs may be any that keep to these rules, and one draw needn't show every extreme that they name: `cluster_ids`: within one head, the 256 tokens of one index of ctx name one cluster at most 2 times. `positions`: every position appears once.
All inputs are finite; a program needn't handle non-finite values.
Results may differ from a plain program's by a relative error of at most 0.02.
Values may be sent and summed in bfloat16 or wider, within the bound.
No kernel may reach another device: no remote copies, remote signals or barrier semaphores. Data moves between devices by JAX's collectives and lax.ppermute only.
A program may use at most 64 MiB of HBM per device.

v0:
```python
import jax
import jax.numpy as jnp
from jax import lax
from jax.sharding import PartitionSpec as P

CLUSTERS = 256
SEND_CAP = 2


def rank_within(member):
    tok_count = member.shape[1]
    matches = member[:, :, None] == member[:, None, :]
    earlier = lax.broadcasted_iota(jnp.int32, (tok_count, tok_count), 0) > lax.broadcasted_iota(
        jnp.int32, (tok_count, tok_count), 1
    )
    return jnp.sum(jnp.logical_and(matches, earlier[None]), axis=2, dtype=jnp.int32)


def weights_of(query_block, key_block, slot_pos, factor):
    scores = (
        jnp.einsum("urd,ujd->urj", query_block, key_block, preferred_element_type=jnp.float32)
        * factor
    )
    allowed = jnp.logical_and(
        slot_pos[:, None, :] >= 0, slot_pos[:, None, :] <= slot_pos[:, :, None]
    )
    scores = jnp.where(allowed, scores, -1e30)
    highest = jnp.max(scores, axis=2, keepdims=True)
    exponent = jnp.exp(scores - highest)
    return exponent / jnp.sum(exponent, axis=2, keepdims=True)


def local(queries, key_vectors, value_vectors, norm_gain, upstream, cluster_ids, positions):
    heads, tokens, feature = queries.shape
    n_ctx = lax.axis_size("ctx")
    per_dev = CLUSTERS // n_ctx
    factor = feature ** (-0.5)
    member = cluster_ids[:, :, 0]
    target = member * SEND_CAP + rank_within(member)
    slots = CLUSTERS * SEND_CAP
    mine = slots // n_ctx
    onehot = target[:, None, :] == lax.broadcasted_iota(jnp.int32, (1, slots, 1), 1)
    place = onehot.astype(jnp.bfloat16)

    def to_owner(source):
        placed = jnp.einsum(
            "hst,htd->hsd", place, source, preferred_element_type=jnp.float32
        ).astype(jnp.bfloat16)
        placed = placed.reshape(heads, n_ctx, mine, source.shape[2])
        placed = placed.transpose(1, 0, 2, 3).reshape(n_ctx, heads * mine, source.shape[2])
        return lax.all_to_all(placed, "ctx", 0, 0, tiled=True)

    def from_owner(block):
        back = lax.all_to_all(block, "ctx", 0, 0, tiled=True)
        back = back.reshape(n_ctx, heads, mine, block.shape[2])
        back = back.transpose(1, 0, 2, 3).reshape(heads, slots, block.shape[2])
        return jnp.einsum("hst,hsd->htd", place, back, preferred_element_type=jnp.float32).astype(
            jnp.bfloat16
        )

    def units(recv):
        width = recv.shape[2]
        block = recv.reshape(n_ctx, heads * per_dev, SEND_CAP, width).transpose(1, 0, 2, 3)
        return block.reshape(heads * per_dev, n_ctx * SEND_CAP, width)

    def ununits(block):
        width = block.shape[2]
        recv = block.reshape(heads * per_dev, n_ctx, SEND_CAP, width).transpose(1, 0, 2, 3)
        return recv.reshape(n_ctx, heads * mine, width)

    pos_slots = (
        jnp.sum(jnp.where(onehot, positions[None, None, :] + 1, 0), axis=2, dtype=jnp.int32) - 1
    )
    pos_slots = (
        pos_slots.reshape(heads, n_ctx, mine).transpose(1, 0, 2).reshape(n_ctx, heads * mine)
    )
    pos_recv = lax.all_to_all(pos_slots, "ctx", 0, 0, tiled=True)
    slot_pos = units(pos_recv[:, :, None])[:, :, 0]
    recv = to_owner(jnp.concatenate([queries, key_vectors, value_vectors], axis=2))
    block = units(recv)
    query_own, key_own, value_own = (
        block[:, :, :feature],
        block[:, :, feature : 2 * feature],
        block[:, :, 2 * feature :],
    )
    weights = weights_of(query_own, key_own, slot_pos, factor)
    rounded = weights.astype(jnp.bfloat16)
    out_own = jnp.einsum(
        "urj,ujd->urd", rounded, value_own, preferred_element_type=jnp.float32
    ).astype(jnp.bfloat16)
    attention = from_owner(ununits(out_own)).astype(jnp.float32)
    width_all = heads * feature * lax.axis_size("head")
    gain_full = norm_gain[:, None, :]
    scaled_grad = gain_full * upstream.astype(jnp.float32)
    sums = lax.psum(
        jnp.stack(
            [
                jnp.sum(attention * attention, axis=(0, 2)),
                jnp.sum(scaled_grad * attention, axis=(0, 2)),
            ]
        ),
        "head",
    )
    inverse = lax.rsqrt(sums[0] / width_all + 1e-06)[None, :, None]
    dot_total = sums[1][None, :, None]
    normed_out = (attention * inverse * gain_full).astype(jnp.bfloat16)
    grad_attention = (
        inverse * scaled_grad - attention * inverse * inverse * inverse * dot_total / width_all
    ).astype(jnp.bfloat16)
    grad_block = units(to_owner(grad_attention))
    delta_row = jnp.sum(grad_block.astype(jnp.float32) * out_own.astype(jnp.float32), axis=2)
    grad_value = jnp.einsum(
        "urj,urd->ujd", rounded, grad_block, preferred_element_type=jnp.float32
    ).astype(jnp.bfloat16)
    grad_prob = jnp.einsum(
        "urd,ujd->urj", grad_block, value_own, preferred_element_type=jnp.float32
    )
    grad_score = (factor * weights * (grad_prob - delta_row[:, :, None])).astype(jnp.bfloat16)
    grad_query = jnp.einsum(
        "urj,ujd->urd", grad_score, key_own, preferred_element_type=jnp.float32
    ).astype(jnp.bfloat16)
    grad_key = jnp.einsum(
        "urj,urd->ujd", grad_score, query_own, preferred_element_type=jnp.float32
    ).astype(jnp.bfloat16)
    grads = from_owner(ununits(jnp.concatenate([grad_query, grad_key, grad_value], axis=2)))
    cluster_sums = jnp.sum(key_own.astype(jnp.float32), axis=1)
    cluster_sums = cluster_sums.reshape(heads, per_dev, feature).transpose(1, 0, 2)
    centroids = cluster_sums * lax.rsqrt(
        jnp.mean(cluster_sums * cluster_sums, axis=2, keepdims=True) + 1e-06
    )
    return (
        normed_out,
        grads[:, :, :feature],
        grads[:, :, feature : 2 * feature],
        grads[:, :, 2 * feature :],
        centroids,
    )


def solution(mesh):
    tok = P("head", "ctx", None)
    in_specs = (tok, tok, tok, P("head", None), tok, tok, P("ctx"))
    out_specs = (tok, tok, tok, tok, P("ctx", "head", None))
    return jax.shard_map(local, mesh=mesh, in_specs=in_specs, out_specs=out_specs, check_vma=False)
```

profile of v0, /device:TPU:1, one launch (start us, length us, event | category | flops | bytes accessed | tf_op | source)
XLA Modules:
  0.0 322.7 jit_solution(3992617199061359926)
XLA Ops:
  0.7 0.7 copy.153
  1.4 0.4 convert_reduce_fusion.1
  1.8 0.7 multiply_add_fusion
  2.4 0.7 broadcast_add_fusion.1
  3.1 0.3 select_reduce_fusion
  3.4 0.3 sub.26
  3.7 0.1 copy.96
  3.8 0.7 copy.97
  4.6 20.4 %all-to-all-start = ((s32[128,1,16]{2,1,0:T(1,128)}), s32[128,1,16]{2,1,0:T(1,128)S(1)}, u32[]{:S(2)}, u32[]{:S(2)}) async-start(s32[128,1,16]{2,1,0:T(1,128)} %copy.97), calls=%async_computation | async-start | bytes 131072 | tf_op jit(solution)/shard_map/all_to_all | solution.py:77
  25.0 2.1 fusion.5
  27.1 0.4 reshape.122
  27.5 0.3 copy.104
  27.8 2.1 copy.105
  29.8 10.1 %all-to-all-done = s32[128,1,16]{2,1,0:T(1,128)S(1)} async-done(((s32[128,1,16]{2,1,0:T(1,128)}), s32[128,1,16]{2,1,0:T(1,128)S(1)}, u32[]{:S(2)}, u32[]{:S(2)}) %all-to-all-start) | async-done | bytes 8224 | tf_op jit(solution)/shard_map/all_to_all | solution.py:77
  39.9 6.6 %all-to-all-start.1 = ((bf16[128,16,384]{2,1,0:T(8,128)(2,1)}), bf16[128,16,384]{2,1,0:T(8,128)(2,1)S(1)}, u32[]{:S(2)}, u32[]{:S(2)}) async-start(bf16[128,16,384]{2,1,0:T(8,128)(2,1)} %copy.105), calls=%async_computation.1 | async-start | bytes 3145728 | tf_op jit(solution)/shard_map/all_to_all | solution.py:51
  46.5 0.1 copy.98
  46.6 0.2 copy.99
  46.8 0.1 copy.101
  46.9 0.1 copy.100
  46.9 76.5 %all-to-all-done.1 = bf16[128,16,384]{2,1,0:T(8,128)(2,1)S(1)} async-done(((bf16[128,16,384]{2,1,0:T(8,128)(2,1)}), bf16[128,16,384]{2,1,0:T(8,128)(2,1)S(1)}, u32[]{:S(2)}, u32[]{:S(2)}) %all-to-all-start.1) | async-done | bytes 1572896 | tf_op jit(solution)/shard_map/all_to_all | solution.py:51
  123.4 0.4 copy.106
  123.8 1.6 copy.107
  125.4 0.6 reshape.125
  126.1 2.8 fusion.49
  128.9 2.1 convolution_convert_fusion.4
  131.0 0.0 copy-start.3
  131.0 0.1 copy.109
  131.1 1.2 copy.110
  132.3 8.7 %all-to-all-start.2 = ((bf16[128,16,128]{2,1,0:T(8,128)(2,1)}), bf16[128,16,128]{2,1,0:T(8,128)(2,1)S(1)}, u32[]{:S(2)}, u32[]{:S(2)}) async-start(bf16[128,16,128]{2,1,0:T(8,128)(2,1)} %copy.110), calls=%async_computation.2 | async-start | bytes 1048576 | tf_op jit(solution)/shard_map/all_to_all | solution.py:54
  141.0 0.1 copy.115
  141.2 33.0 %all-to-all-done.2 = bf16[128,16,128]{2,1,0:T(8,128)(2,1)S(1)} async-done(((bf16[128,16,128]{2,1,0:T(8,128)(2,1)}), bf16[128,16,128]{2,1,0:T(8,128)(2,1)S(1)}, u32[]{:S(2)}, u32[]{:S(2)}) %all-to-all-start.2) | async-done | bytes 524320 | tf_op jit(solution)/shard_map/all_to_all | solution.py:54
  174.2 0.1 copy.111
  174.4 0.4 copy.112
  174.8 1.0 multiply_reduce_fusion.2
  175.8 8.7 %psum.7 = f32[2,256]{1,0:T(2,128)S(1)} all-reduce(f32[2,256]{1,0:T(2,128)S(1)} %pad_maximum_fusion.1), channel_id=1, replica_groups=mesh['ctx'=128,'head'=4] {'head'}, use_global_device_ids=true, to_apply=%region_6.7 | all-reduce | flops 512 | bytes 4096 | tf_op jit(solution)/shard_map/psum | solution.py:95
  184.5 0.8 convolution_convert_fusion
  185.3 0.1 copy.118
  185.4 0.0 copy-start.5
  185.5 0.3 copy.119
  185.8 42.3 %all_to_all.29 = bf16[128,16,128]{2,1,0:T(8,128)(2,1)S(1)} all-to-all(bf16[128,16,128]{2,1,0:T(8,128)(2,1)S(1)} %copy.119), channel_id=1, replica_groups=mesh['ctx'=128,'head'=4] {'ctx'}, dimensions={0} | all-to-all | bytes 1048576 | tf_op jit(solution)/shard_map/all_to_all | solution.py:51
  228.1 0.1 copy.120
  228.3 0.5 copy.121
  228.8 0.5 convolution_convert_fusion.1
  229.3 0.3 multiply_reduce_fusion
  229.7 0.5 multiply_convert_fusion
  230.2 0.5 convolution_convert_fusion.2
  230.7 0.4 convolution_convert_fusion.3
  231.1 0.1 pad_maximum_fusion
  231.2 1.3 copy.129
  232.5 0.4 copy.130
  232.9 2.1 copy.131
  235.0 7.3 %all-to-all-start.4 = ((bf16[128,16,384]{2,1,0:T(8,128)(2,1)}), bf16[128,16,384]{2,1,0:T(8,128)(2,1)S(1)}, u32[]{:S(2)}, u32[]{:S(2)}) async-start(bf16[128,16,384]{2,1,0:T(8,128)(2,1)} %copy.131), calls=%async_computation.4 | async-start | bytes 3145728 | tf_op jit(solution)/shard_map/all_to_all | solution.py:54
  242.3 1.1 convert_reduce_fusion
  243.4 0.1 multiply_reduce_fusion.3
  243.5 0.1 broadcast_multiply_fusion
  243.6 0.6 copy.135
  244.2 0.1 multiply_convert_fusion.1
  244.3 0.8 copy.134
  245.1 73.9 %all-to-all-done.4 = bf16[128,16,384]{2,1,0:T(8,128)(2,1)S(1)} async-done(((bf16[128,16,384]{2,1,0:T(8,128)(2,1)}), bf16[128,16,384]{2,1,0:T(8,128)(2,1)S(1)}, u32[]{:S(2)}, u32[]{:S(2)}) %all-to-all-start.4) | async-done | bytes 1572896 | tf_op jit(solution)/shard_map/all_to_all | solution.py:54
  319.0 0.4 copy.132
  319.4 1.2 copy.133
  320.6 0.4 reshape.137
  321.0 0.8 fusion.6
  321.8 0.9 fusion.47
  (16 shorter events, 0.1 us)
Async XLA Ops:
  4.6 35.4 %all-to-all-start = ((s32[128,1,16]{2,1,0:T(1,128)}), s32[128,1,16]{2,1,0:T(1,128)S(1)}, u32[]{:S(2)}, u32[]{:S(2)}) async-start(s32[128,1,16]{2,1,0:T(1,128)} %copy.97), calls=%async_computation | async-start | bytes 131072 | tf_op jit(solution)/shard_map/all_to_all | solution.py:77
  39.9 83.5 %all-to-all-start.1 = ((bf16[128,16,384]{2,1,0:T(8,128)(2,1)}), bf16[128,16,384]{2,1,0:T(8,128)(2,1)S(1)}, u32[]{:S(2)}, u32[]{:S(2)}) async-start(bf16[128,16,384]{2,1,0:T(8,128)(2,1)} %copy.105), calls=%async_computation.1 | async-start | bytes 3145728 | tf_op jit(solution)/shard_map/all_to_all | solution.py:51
  126.1 104.6 %copy-start = (bf16[8,256,384]{2,1,0:T(8,128)(2,1)}, bf16[8,256,384]{2,1,0:T(8,128)(2,1)S(1)}, u32[]{:S(2)}) copy-start(bf16[8,256,384]{2,1,0:T(8,128)(2,1)S(1)} %reshape.125) | copy-start | bytes 4718596
  131.0 10.0 %copy-start.3 = (bf16[4,256,128]{2,1,0:T(8,128)(2,1)S(1)}, bf16[4,256,128]{2,1,0:T(8,128)(2,1)}, u32[]{:S(2)}) copy-start(bf16[4,256,128]{2,1,0:T(8,128)(2,1)} %param.11) | copy-start | bytes 786436
  132.3 42.5 %copy-start.4 = (f32[4,128]{1,0:T(4,128)S(1)}, f32[4,128]{1,0:T(4,128)}, u32[]{:S(2)}) copy-start(f32[4,128]{1,0:T(4,128)} %param.10) | copy-start | bytes 6148
  132.3 41.9 %all-to-all-start.2 = ((bf16[128,16,128]{2,1,0:T(8,128)(2,1)}), bf16[128,16,128]{2,1,0:T(8,128)(2,1)S(1)}, u32[]{:S(2)}, u32[]{:S(2)}) async-start(bf16[128,16,128]{2,1,0:T(8,128)(2,1)} %copy.110), calls=%async_computation.2 | async-start | bytes 1048576 | tf_op jit(solution)/shard_map/all_to_all | solution.py:54
  175.7 9.6 %copy-start.1 = (f32[4,256,128]{1,2,0:T(8,128)}, f32[4,256,128]{1,2,0:T(8,128)S(1)}, u32[]{:S(2)}) copy-start(f32[4,256,128]{1,2,0:T(8,128)S(1)} %get-tuple-element.34) | copy-start | bytes 1572868
  185.4 43.4 %copy-start.5 = (f32[8,256,256]{1,2,0:T(8,128)S(1)}, f32[8,256,256]{1,2,0:T(8,128)}, u32[]{:S(2)}) copy-start(f32[8,256,256]{1,2,0:T(8,128)} %get-tuple-element.33) | copy-start | bytes 6291460
  235.0 9.2 %copy-start.2 = (f32[4,256,128]{1,2,0:T(8,128)S(1)}, f32[4,256,128]{1,2,0:T(8,128)}, u32[]{:S(2)}) copy-start(f32[4,256,128]{1,2,0:T(8,128)} %copy-done.1) | copy-start | bytes 1572868
  235.0 84.1 %all-to-all-start.4 = ((bf16[128,16,384]{2,1,0:T(8,128)(2,1)}), bf16[128,16,384]{2,1,0:T(8,128)(2,1)S(1)}, u32[]{:S(2)}, u32[]{:S(2)}) async-start(bf16[128,16,384]{2,1,0:T(8,128)(2,1)} %copy.131), calls=%async_computation.4 | async-start | bytes 3145728 | tf_op jit(solution)/shard_map/all_to_all | solution.py:54
where the time goes:
time: 323 us
  waiting for transfers between devices  194 us (60%)
  blocking collectives  51 us (16%)
  starting transfers between devices  43 us (13%)
  local copies, waits for them, and re-layouts  18.7 us (6%)
  matrix products  11.4 us (4%)
  other arithmetic  4.03 us (1%)
    all_to_all x2, waiting for transfers between devices, from_owner(): back = lax.all_to_all(block, 'ctx', 0, 0, tiled=True)  107 us
    all_to_all x1, waiting for transfers between devices, to_owner(): return lax.all_to_all(placed, 'ctx', 0, 0, tiled=True)  76.5 us
    all_to_all x1, blocking collectives, to_owner(): return lax.all_to_all(placed, 'ctx', 0, 0, tiled=True)  42.3 us
    all_to_all x1, starting transfers between devices, local(): pos_recv = lax.all_to_all(pos_slots, 'ctx', 0, 0, tiled=True)  20.4 us
    all_to_all x2, starting transfers between devices, from_owner(): back = lax.all_to_all(block, 'ctx', 0, 0, tiled=True)  16 us
    all_to_all x1, waiting for transfers between devices, local(): pos_recv = lax.all_to_all(pos_slots, 'ctx', 0, 0, tiled=True)  10.1 us
    psum x1, blocking collectives, local(): lax.psum(jnp.stack([jnp.sum(attention * attention, axis=(0, 2)), jnp.sum(...  8.73 us
    all_to_all x1, starting transfers between devices, to_owner(): return lax.all_to_all(placed, 'ctx', 0, 0, tiled=True)  6.58 us
  transfers between devices with their start and end apart: 4, of which 4 were waited for; matrix products, arithmetic and copies ran while one was open for 3% of the time, Pallas kernels for 0%

commit v1 on v0

--- a/solution.py
+++ b/solution.py
@@ -92,14 +92,17 @@
     width_all = heads * feature * lax.axis_size("head")
     gain_full = norm_gain[:, None, :]
     scaled_grad = gain_full * upstream.astype(jnp.float32)
-    sums = lax.psum(
-        jnp.stack(
-            [
-                jnp.sum(attention * attention, axis=(0, 2)),
-                jnp.sum(scaled_grad * attention, axis=(0, 2)),
-            ]
+    sums = jnp.sum(
+        lax.all_gather(
+            jnp.stack(
+                [
+                    jnp.sum(attention * attention, axis=(0, 2)),
+                    jnp.sum(scaled_grad * attention, axis=(0, 2)),
+                ]
+            ),
+            "head",
         ),
-        "head",
+        axis=0,
     )
     inverse = lax.rsqrt(sums[0] / width_all + 1e-06)[None, :, None]
     dot_total = sums[1][None, :, None]

time: 323 us -> 324 us (level)
    psum x1 -> x0, blocking collectives: 8.73 us -> none  [local(): lax.psum(jnp.stack([jnp.sum(attention * attention, axis=(0, 2)), jnp.sum(...]
    all_gather x0 -> x1, blocking collectives: none -> 8.6 us  [local(): lax.all_gather(jnp.stack([jnp.sum(attention * attention, axis=(0, 2)), jn...]
where the time goes in v1:
time: 324 us; the launch traced here: 323 us
  waiting for transfers between devices  194 us (60%)
  blocking collectives  51.5 us (16%)
  starting transfers between devices  43 us (13%)
  local copies, waits for them, and re-layouts  18.7 us (6%)
  matrix products  11.4 us (4%)
  other arithmetic  4.04 us (1%)
    all_to_all x2, waiting for transfers between devices, from_owner(): back = lax.all_to_all(block, 'ctx', 0, 0, tiled=True)  107 us
    all_to_all x1, waiting for transfers between devices, to_owner(): return lax.all_to_all(placed, 'ctx', 0, 0, tiled=True)  76.5 us
    all_to_all x1, blocking collectives, to_owner(): return lax.all_to_all(placed, 'ctx', 0, 0, tiled=True)  42.9 us
    all_to_all x1, starting transfers between devices, local(): pos_recv = lax.all_to_all(pos_slots, 'ctx', 0, 0, tiled=True)  20.4 us
    all_to_all x2, starting transfers between devices, from_owner(): back = lax.all_to_all(block, 'ctx', 0, 0, tiled=True)  16 us
    all_to_all x1, waiting for transfers between devices, local(): pos_recv = lax.all_to_all(pos_slots, 'ctx', 0, 0, tiled=True)  10.1 us
    all_gather x1, blocking collectives, local(): lax.all_gather(jnp.stack([jnp.sum(attention * attention, axis=(0, 2)), jn...  8.6 us
    all_to_all x1, starting transfers between devices, to_owner(): return lax.all_to_all(placed, 'ctx', 0, 0, tiled=True)  6.58 us
  transfers between devices with their start and end apart: 4, of which 4 were waited for; matrix products, arithmetic and copies ran while one was open for 3% of the time, Pallas kernels for 0%

profile of v1, /device:TPU:1, one launch (start us, length us, event | category | flops | bytes accessed | tf_op | source)
XLA Modules:
  0.0 323.3 jit_solution(7042655276126263743)
XLA Ops:
  0.7 0.7 copy.153
  1.4 0.4 convert_reduce_fusion.1
  1.8 0.7 multiply_add_fusion
  2.4 0.7 broadcast_add_fusion.1
  3.1 0.3 select_reduce_fusion
  3.4 0.3 sub.26
  3.7 0.1 copy.96
  3.8 0.7 copy.97
  4.6 20.4 %all-to-all-start = ((s32[128,1,16]{2,1,0:T(1,128)}), s32[128,1,16]{2,1,0:T(1,128)S(1)}, u32[]{:S(2)}, u32[]{:S(2)}) async-start(s32[128,1,16]{2,1,0:T(1,128)} %copy.97), calls=%async_computation | async-start | bytes 131072 | tf_op jit(solution)/shard_map/all_to_all | solution.py:77
  25.0 2.1 fusion.5
  27.1 0.4 reshape.122
  27.5 0.3 copy.104
  27.8 2.1 copy.105
  29.8 10.1 %all-to-all-done = s32[128,1,16]{2,1,0:T(1,128)S(1)} async-done(((s32[128,1,16]{2,1,0:T(1,128)}), s32[128,1,16]{2,1,0:T(1,128)S(1)}, u32[]{:S(2)}, u32[]{:S(2)}) %all-to-all-start) | async-done | bytes 8224 | tf_op jit(solution)/shard_map/all_to_all | solution.py:77
  39.9 6.6 %all-to-all-start.1 = ((bf16[128,16,384]{2,1,0:T(8,128)(2,1)}), bf16[128,16,384]{2,1,0:T(8,128)(2,1)S(1)}, u32[]{:S(2)}, u32[]{:S(2)}) async-start(bf16[128,16,384]{2,1,0:T(8,128)(2,1)} %copy.105), calls=%async_computation.1 | async-start | bytes 3145728 | tf_op jit(solution)/shard_map/all_to_all | solution.py:51
  46.5 0.1 copy.98
  46.6 0.2 copy.99
  46.8 0.1 copy.101
  46.9 0.1 copy.100
  46.9 76.5 %all-to-all-done.1 = bf16[128,16,384]{2,1,0:T(8,128)(2,1)S(1)} async-done(((bf16[128,16,384]{2,1,0:T(8,128)(2,1)}), bf16[128,16,384]{2,1,0:T(8,128)(2,1)S(1)}, u32[]{:S(2)}, u32[]{:S(2)}) %all-to-all-start.1) | async-done | bytes 1572896 | tf_op jit(solution)/shard_map/all_to_all | solution.py:51
  123.4 0.4 copy.106
  123.8 1.6 copy.107
  125.4 0.6 reshape.125
  126.1 0.0 copy-start
  126.1 2.8 fusion.49
  128.9 2.1 convolution_convert_fusion.4
  131.0 0.0 copy-start.3
  131.0 0.1 copy.109
  131.1 1.2 copy.110
  132.3 8.7 %all-to-all-start.2 = ((bf16[128,16,128]{2,1,0:T(8,128)(2,1)}), bf16[128,16,128]{2,1,0:T(8,128)(2,1)S(1)}, u32[]{:S(2)}, u32[]{:S(2)}) async-start(bf16[128,16,128]{2,1,0:T(8,128)(2,1)} %copy.110), calls=%async_computation.2 | async-start | bytes 1048576 | tf_op jit(solution)/shard_map/all_to_all | solution.py:54
  141.0 0.1 copy.115
  141.2 33.0 %all-to-all-done.2 = bf16[128,16,128]{2,1,0:T(8,128)(2,1)S(1)} async-done(((bf16[128,16,128]{2,1,0:T(8,128)(2,1)}), bf16[128,16,128]{2,1,0:T(8,128)(2,1)S(1)}, u32[]{:S(2)}, u32[]{:S(2)}) %all-to-all-start.2) | async-done | bytes 524320 | tf_op jit(solution)/shard_map/all_to_all | solution.py:54
  174.2 0.1 copy.111
  174.4 0.4 copy.112
  174.8 1.0 multiply_reduce_fusion.2
  175.8 8.6 %all-gather.1 = f32[4,2,256]{2,1,0:T(2,128)S(1)} all-gather(f32[1,2,256]{2,1,0:T(2,128)S(1)} %maximum_bitcast_fusion), channel_id=2, replica_groups=mesh['ctx'=128,'head'=4] {'head'}, dimensions={0}, use_global_device_ids=true | all-gather | bytes 10240 | tf_op jit(solution)/shard_map/all_gather | solution.py:96
  184.4 0.8 convolution_convert_fusion
  185.2 0.1 copy.118
  185.3 0.3 copy.119
  185.7 42.9 %all_to_all.29 = bf16[128,16,128]{2,1,0:T(8,128)(2,1)S(1)} all-to-all(bf16[128,16,128]{2,1,0:T(8,128)(2,1)S(1)} %copy.119), channel_id=1, replica_groups=mesh['ctx'=128,'head'=4] {'ctx'}, dimensions={0} | all-to-all | bytes 1048576 | tf_op jit(solution)/shard_map/all_to_all | solution.py:51
  228.6 0.1 copy.120
  228.8 0.5 copy.121
  229.3 0.5 convolution_convert_fusion.1
  229.8 0.3 multiply_reduce_fusion
  230.2 0.5 multiply_convert_fusion
  230.7 0.5 convolution_convert_fusion.2
  231.2 0.4 convolution_convert_fusion.3
  231.6 0.1 pad_maximum_fusion
  231.7 1.3 copy.129
  233.0 0.4 copy.130
  233.4 2.1 copy.131
  235.5 7.3 %all-to-all-start.4 = ((bf16[128,16,384]{2,1,0:T(8,128)(2,1)}), bf16[128,16,384]{2,1,0:T(8,128)(2,1)S(1)}, u32[]{:S(2)}, u32[]{:S(2)}) async-start(bf16[128,16,384]{2,1,0:T(8,128)(2,1)} %copy.131), calls=%async_computation.4 | async-start | bytes 3145728 | tf_op jit(solution)/shard_map/all_to_all | solution.py:54
  242.8 1.1 convert_reduce_fusion
  243.9 0.1 multiply_reduce_fusion.3
  244.0 0.1 broadcast_multiply_fusion
  244.1 0.6 copy.135
  244.7 0.1 multiply_convert_fusion.1
  244.8 0.8 copy.134
  245.7 73.9 %all-to-all-done.4 = bf16[128,16,384]{2,1,0:T(8,128)(2,1)S(1)} async-done(((bf16[128,16,384]{2,1,0:T(8,128)(2,1)}), bf16[128,16,384]{2,1,0:T(8,128)(2,1)S(1)}, u32[]{:S(2)}, u32[]{:S(2)}) %all-to-all-start.4) | async-done | bytes 1572896 | tf_op jit(solution)/shard_map/all_to_all | solution.py:54
  319.5 0.4 copy.132
  319.9 1.2 copy.133
  321.1 0.4 reshape.137
  321.6 0.8 fusion.6
  322.3 0.9 fusion.47
  (17 shorter events, 0.1 us)
Async XLA Ops:
  4.6 35.4 %all-to-all-start = ((s32[128,1,16]{2,1,0:T(1,128)}), s32[128,1,16]{2,1,0:T(1,128)S(1)}, u32[]{:S(2)}, u32[]{:S(2)}) async-start(s32[128,1,16]{2,1,0:T(1,128)} %copy.97), calls=%async_computation | async-start | bytes 131072 | tf_op jit(solution)/shard_map/all_to_all | solution.py:77
  39.9 83.5 %all-to-all-start.1 = ((bf16[128,16,384]{2,1,0:T(8,128)(2,1)}), bf16[128,16,384]{2,1,0:T(8,128)(2,1)S(1)}, u32[]{:S(2)}, u32[]{:S(2)}) async-start(bf16[128,16,384]{2,1,0:T(8,128)(2,1)} %copy.105), calls=%async_computation.1 | async-start | bytes 3145728 | tf_op jit(solution)/shard_map/all_to_all | solution.py:51
  126.1 105.1 %copy-start = (bf16[8,256,384]{2,1,0:T(8,128)(2,1)}, bf16[8,256,384]{2,1,0:T(8,128)(2,1)S(1)}, u32[]{:S(2)}) copy-start(bf16[8,256,384]{2,1,0:T(8,128)(2,1)S(1)} %reshape.125) | copy-start | bytes 4718596
  131.0 10.0 %copy-start.3 = (bf16[4,256,128]{2,1,0:T(8,128)(2,1)S(1)}, bf16[4,256,128]{2,1,0:T(8,128)(2,1)}, u32[]{:S(2)}) copy-start(bf16[4,256,128]{2,1,0:T(8,128)(2,1)} %param.11) | copy-start | bytes 786436
  132.3 42.5 %copy-start.4 = (f32[4,128]{1,0:T(4,128)S(1)}, f32[4,128]{1,0:T(4,128)}, u32[]{:S(2)}) copy-start(f32[4,128]{1,0:T(4,128)} %param.10) | copy-start | bytes 6148
  132.3 41.9 %all-to-all-start.2 = ((bf16[128,16,128]{2,1,0:T(8,128)(2,1)}), bf16[128,16,128]{2,1,0:T(8,128)(2,1)S(1)}, u32[]{:S(2)}, u32[]{:S(2)}) async-start(bf16[128,16,128]{2,1,0:T(8,128)(2,1)} %copy.110), calls=%async_computation.2 | async-start | bytes 1048576 | tf_op jit(solution)/shard_map/all_to_all | solution.py:54
  175.7 9.5 %copy-start.1 = (f32[4,256,128]{1,2,0:T(8,128)}, f32[4,256,128]{1,2,0:T(8,128)S(1)}, u32[]{:S(2)}) copy-start(f32[4,256,128]{1,2,0:T(8,128)S(1)} %get-tuple-element.34) | copy-start | bytes 1572868
  185.3 44.0 %copy-start.5 = (f32[8,256,256]{1,2,0:T(8,128)S(1)}, f32[8,256,256]{1,2,0:T(8,128)}, u32[]{:S(2)}) copy-start(f32[8,256,256]{1,2,0:T(8,128)} %get-tuple-element.33) | copy-start | bytes 6291460
  235.5 9.2 %copy-start.2 = (f32[4,256,128]{1,2,0:T(8,128)S(1)}, f32[4,256,128]{1,2,0:T(8,128)}, u32[]{:S(2)}) copy-start(f32[4,256,128]{1,2,0:T(8,128)} %copy-done.1) | copy-start | bytes 1572868
  235.5 84.1 %all-to-all-start.4 = ((bf16[128,16,384]{2,1,0:T(8,128)(2,1)}), bf16[128,16,384]{2,1,0:T(8,128)(2,1)S(1)}, u32[]{:S(2)}, u32[]{:S(2)}) async-start(bf16[128,16,384]{2,1,0:T(8,128)(2,1)} %copy.131), calls=%async_computation.4 | async-start | bytes 3145728 | tf_op jit(solution)/shard_map/all_to_all | solution.py:54
